TPU v7x, 32 devices: a whole 2x2x4 slice. The times are simulated.
32 devices in a mesh: grp: 2 (over y), row: 4 (over z), col: 2 (over x), sub: 2 (over core).
Axes of the slice: x: 2, y: 2, z: 4, core: 2. Of those that a mesh axis runs over, the one named last changes fastest.
Arguments:
- sigma_parent: float32 [6, 4, 256, 6, 2, 256], P('grp', 'row', 'sub', None, 'col'), parts along dimension 0, may hold values from -10 to 10
- panel: float32 [4, 4, 256, 256], P(('grp', 'col'), 'row', 'sub'), parts along dimension 0, may hold values from -0.6 to 0.6
- diag_factor: float32 [4, 256, 256], P(('grp', 'col')), parts along dimension 0, may hold values from -1 to 3, as said below
- frontier: int32 [4, 4], P('grp'), parts along dimension 0, may hold values from 0 to 11, as said below
Outputs:
- sigma_cross: float32 [4, 4, 256, 256], P(('grp', 'col'), 'row', 'sub'), parts along dimension 0
- sigma_diag: float32 [4, 256, 256], P(('grp', 'col')), parts along dimension 0
There are 2 independent parts, one for each index of `grp`. A program takes and returns all parts, laid end to end along the dimension named above; each array names one. Nothing has to cross between parts.
Inputs may be any that keep to these rules, and one draw needn't show every extreme that they name: `frontier`: each row holds 4 different parent block numbers in increasing order; in each row at most 3 of them share one remainder modulo the number of block-column owners, and exactly 3 do for some remainder. `diag_factor`: lower triangular, every diagonal entry at least 1.
All inputs are finite; a program needn't handle non-finite values.
Results may differ from a plain program's by a relative error of at most 0.000071.
Values sent between devices are 32-bit elements; how exact they have to be, the bound alone decides.
A program may use at most 64 MiB of HBM per device.

v0:
```python
import jax
import jax.numpy as jnp
from jax import lax
from jax.sharding import PartitionSpec as P

HIGHEST = lax.Precision.HIGHEST


def take_rows(table_rows, where_rows):
    return jnp.take(table_rows, where_rows, axis=0)


def per_device(sigma_parent, panel, diag_factor, frontier):
    row_count = lax.axis_size("row")
    col_count = lax.axis_size("col")
    row_index = lax.axis_index("row")
    col_index = lax.axis_index("col")
    kid_count, rows_here, half_rows, blk_width = panel.shape
    par_rows = sigma_parent.shape[0]
    par_cols = sigma_parent.shape[3]
    front_len = frontier.shape[1]
    slot_count = front_len // col_count + 1
    identity = jnp.broadcast_to(
        jnp.eye(blk_width, dtype=jnp.float32), (kid_count, blk_width, blk_width)
    )
    inverse = lax.linalg.triangular_solve(diag_factor, identity, left_side=True, lower=True)
    update = jnp.einsum("krhb,kbc->krhc", panel, inverse, precision=HIGHEST)
    whole_panel = lax.all_gather(update, "row", axis=1, tiled=True)
    my_struct = lax.dynamic_slice_in_dim(frontier, col_index * kid_count, kid_count, 0)
    col_owner = frontier % col_count
    onehot_col = (col_owner[:, :, None] == jnp.arange(col_count)[None, None, :]).astype(jnp.int32)
    position = jnp.cumsum(onehot_col, axis=1) - 1
    slot_hit = (position[..., None] == jnp.arange(slot_count)) & (onehot_col[..., None] == 1)
    picker = slot_hit.astype(jnp.float32)
    my_picker = lax.dynamic_slice_in_dim(picker, col_index * kid_count, kid_count, 0)
    outgoing = jnp.einsum("kacm,kahb->ckmhb", my_picker, whole_panel, precision=HIGHEST)
    incoming = lax.all_to_all(outgoing, "col", split_axis=0, concat_axis=0, tiled=True)
    blocks = lax.all_gather(incoming, "sub", axis=3, tiled=True)
    blocks = blocks.reshape(col_count * kid_count, slot_count, blk_width, blk_width)
    mine_hits = lax.dynamic_index_in_dim(picker, col_index, 2, keepdims=False)
    local_col = frontier // col_count
    column_hit = (local_col[..., None] == jnp.arange(par_cols)).astype(jnp.float32)
    spread_map = jnp.einsum("kam,kaj->kmj", mine_hits, column_hit, precision=HIGHEST)
    parent_local = sigma_parent.reshape(par_rows, half_rows, par_cols, blk_width)
    selected = jnp.einsum("kmj,ihjx->kihmx", spread_map, parent_local, precision=HIGHEST)
    reduced = lax.psum_scatter(
        jnp.einsum("kihmx,kmxy->kihy", selected, blocks, precision=HIGHEST),
        "col",
        scatter_dimension=0,
        tiled=True,
    )
    wanted = lax.dynamic_slice_in_dim(my_struct, row_index * rows_here, rows_here, 1)
    collected = lax.all_gather(reduced[:, None], "row", axis=1, tiled=True)
    flat_rows = collected.reshape(kid_count, row_count * par_rows, half_rows, blk_width)
    pick_rows = wanted % row_count * par_rows + wanted // row_count
    picked = jax.vmap(take_rows)(flat_rows, pick_rows)
    diag_part = jnp.einsum("krhb,krhc->kbc", update, picked, precision=HIGHEST)
    summed = lax.psum(diag_part, ("row", "sub"))
    diag_out = jnp.einsum("kab,kac->kbc", inverse, inverse, precision=HIGHEST) + summed
    return (-picked, diag_out)


def solution(mesh):
    in_specs = (
        P("grp", "row", "sub", None, "col", None),
        P(("grp", "col"), "row", "sub", None),
        P(("grp", "col"), None, None),
        P("grp", None),
    )
    out_specs = (P(("grp", "col"), "row", "sub", None), P(("grp", "col"), None, None))
    return jax.shard_map(
        per_device, mesh=mesh, in_specs=in_specs, out_specs=out_specs, check_vma=False
    )
```

profile of v0, /device:TPU:1, one launch (start us, length us, event | category | flops | bytes accessed | tf_op | source)
XLA Modules:
  0.0 202.0 jit_solution(5876648810269600243)
XLA Ops:
  7.2 0.0 copy-start
  7.2 0.0 all-gather.5.cloned.1.call-start
  7.3 0.7 and_select_fusion
  8.0 0.4 reduce_window_sum.11
  8.4 1.0 fusion.18
  9.3 0.1 triangular_solve.62
  9.4 3.9 %while.2 = (s32[]{:T(128)}, f32[1,256,256]{2,1,0:T(8,128)S(1)}, s32[2,2]{1,0:T(2,128)S(1)}, f32[2,1,128,128]{3,2,1,0:T(8,128)S(1)}, s32[]{:T(128)}) while((s32[]{:T(128)}, f32[1,256,256]{2,1,0:T(8,128)S(1)}, s32[2,2]{1,0:T(2,128)S(1)}, f32[2,1,128,128]{3,2,1,0:T(8,128)S(1)}, s32[]{:T(128)}) %tuple.30), condition=%wide.while_cond, body=%wide.while_body.sunk | while | flops 2 | bytes 131189 | solution.py:26
  9.4 0.6 fusion.45
  10.0 1.4 bitcast_dynamic-update-slice_fusion.2
  11.4 0.6 fusion.45
  12.0 1.4 bitcast_dynamic-update-slice_fusion.2
  13.3 19.7 %custom-call.3 = f32[1,2,128,128]{2,3,1,0:T(8,128)S(1)} custom-call(f32[1,2,128,128]{3,2,1,0:T(8,128)S(1)} %bitcast.108), custom_call_target="InvertDiagBlocksLowerTriangular" | custom-call | tf_op jit(solution)/shard_map/triangular_solve | solution.py:26
  33.0 0.3 fusion.22
  33.3 0.3 fusion.17
  33.6 0.3 convolution_bitcast_fusion.3
  33.9 0.0 copy-start.1
  33.9 0.0 copy-done
  33.9 0.6 fusion.19
  34.5 0.0 copy-done.1
  34.5 15.3 %all-gather = f32[512,256]{0,1:T(8,128)S(1)} all-gather(f32[128,256]{0,1:T(8,128)S(1)} %bitcast.105), channel_id=2, replica_groups=mesh['grp'=2,'row'=4,'col'=2,'sub'=2] {'row'}, dimensions={0}, use_global_device_ids=true | all-gather | bytes 655360 | tf_op jit(solution)/shard_map/all_gather | solution.py:28
  49.8 0.2 reshape.140
  50.0 0.2 copy.24
  50.2 0.1 fusion.26
  50.3 1.0 convolution_bitcast_fusion
  51.4 0.3 copy.18
  51.6 11.0 %all_to_all.5 = f32[2,1,3,128,256]{4,3,2,1,0:T(8,128)S(1)} all-to-all(f32[2,1,3,128,256]{4,3,2,1,0:T(8,128)S(1)} %copy.18), channel_id=1, replica_groups=mesh['grp'=2,'row'=4,'col'=2,'sub'=2] {'col'}, dimensions={0} | all-to-all | bytes 1572864 | tf_op jit(solution)/shard_map/all_to_all | solution.py:37
  62.6 1.5 copy.19
  64.1 0.0 all-gather.5.cloned.1.call-update
  64.1 0.2 reduce-scatter.2.cloned.1.call-start
  64.4 0.2 convolution_bitcast_fusion.5
  64.5 5.8 %fusion.5 = f32[2,3,128,3,256]{4,3,2,1,0:T(4,128)S(1)} fusion(f32[2,3,6,1,1]{2,1,4,3,0:T(4,128)S(1)} %convolution_bitcast_fusion.5, f32[3,1,128,6,1,256]{5,4,3,2,1,0:T(1,128)} %param.4), kind=kOutput, calls=%fused_computation.7 | convolution fusion | flops 42467328 | bytes 4718736 | tf_op jit(solution)/shard_map/kmj,ihjx->kihmx/dot_general | solution.py:45
  70.4 0.0 copy-start.3
  70.4 6.0 %all-gather.5.cloned.1.call-done = f32[2,1,3,256,256]{4,0,2,1,3:T(2,128)} async-done(((f32[2,1,3,128,256]{4,0,2,1,3:T(2,128)}), f32[2,1,3,256,256]{4,0,2,1,3:T(2,128)}) %all-gather.5.cloned.1.call-update) | async-done | bytes 1572880 | tf_op jit(solution)/shard_map/all_gather | solution.py:38
  76.3 4.7 %fusion.10 = f32[2,3,128,256]{3,2,1,0:T(8,128)} fusion(f32[2,1,3,256,256]{4,0,2,1,3:T(2,128)} %all-gather.5.cloned.1.call-done, f32[2,3,128,3,256]{4,3,2,1,0:T(4,128)S(1)} %fusion.5), kind=kOutput, calls=%fused_computation.11 | convolution fusion | flops 1811939328 | bytes 4718592 | tf_op jit(solution)/shard_map/kihmx,kmxy->kihy/dot_general | solution.py:47
  81.0 0.0 reduce-scatter.2.cloned.1.call-update
  81.1 0.0 all-gather.7.cloned.1.call-start
  81.1 18.3 %reduce-scatter.2.cloned.1.call-done = f32[1,3,128,256]{3,2,1,0:T(8,128)} async-done(((f32[2,3,128,256]{3,2,1,0:T(8,128)}), f32[1,3,128,256]{3,2,1,0:T(8,128)}) %reduce-scatter.2.cloned.1.call-update) | async-done | bytes 393232 | tf_op jit(solution)/shard_map/reduce_scatter | solution.py:46
  99.5 0.0 all-gather.7.cloned.1.call-update
  99.5 0.0 all-reduce.2.cloned.1.call-start
  99.5 0.6 dynamic_slice.11
  102.8 0.1 pad_bitcast_fusion
  102.8 0.6 slice.37
  103.5 34.6 %all-gather.7.cloned.1.call-done = f32[4,3,128,256]{3,2,1,0:T(8,128)} async-done(((f32[1,3,128,256]{3,2,1,0:T(8,128)}), f32[4,3,128,256]{3,2,1,0:T(8,128)}) %all-gather.7.cloned.1.call-update) | async-done | bytes 1572880 | tf_op jit(solution)/shard_map/all_gather | solution.py:53
  138.1 2.6 %convolution_bitcast_fusion.2 = f32[1,256,256]{2,1,0:T(8,128)} fusion(f32[256,128]{1,0:T(8,128)S(1)} %fusion.19, f32[1,12,128,256]{3,2,1,0:T(8,128)} %bitcast.106, s32[]{:T(128)} %bitcast.33, pred[]{:T(512)} %bitcast.1), kind=kOutput, calls=%fused_computation.13 | convolution fusion | flops 100696064 | bytes 525312 | tf_op jit(solution)/shard_map/krhb,krhc->kbc/dot_general | solution.py:57
  140.8 0.0 all-reduce.2.cloned.1.call-update
  140.8 2.2 %fusion.23 = f32[1,1,128,256]{3,2,1,0:T(8,128)} fusion(f32[1,12,128,256]{3,2,1,0:T(8,128)} %bitcast.107, s32[]{:T(128)} %bitcast.33, pred[]{:T(512)} %bitcast.1), kind=kLoop, calls=%fused_computation.30 | loop fusion | flops 65536 | bytes 262149 | tf_op jit(solution)/shard_map/neg | solution.py:60
  143.0 50.2 %all-reduce.2.cloned.1.call-done = f32[1,256,256]{2,1,0:T(8,128)} async-done(((f32[1,256,256]{2,1,0:T(8,128)}), f32[1,256,256]{2,1,0:T(8,128)}) %all-reduce.2.cloned.1.call-update) | async-done | bytes 262160 | tf_op jit(solution)/shard_map/psum | solution.py:58
  193.3 2.2 %fusion.15 = f32[1,256,256]{2,1,0:T(8,128)} fusion(f32[1,256,256]{2,1,0:T(8,128)} %all-reduce.2.cloned.1.call-done, f32[1,128,256]{2,1,0:T(8,128)S(1)} %copy-done.2, f32[1,128,256]{2,1,0:T(8,128)S(1)} %bitcast.104), kind=kOutput, calls=%fused_computation.14 | convolution fusion | flops 201457664 | bytes 786432 | tf_op jit(solution)/shard_map/kab,kac->kbc/dot_general | solution.py:59
  (10 shorter events, 0.1 us)
Async XLA Ops:
  7.2 26.7 %copy-start = (f32[1,1,128,256]{3,2,1,0:T(8,128)S(1)}, f32[1,1,128,256]{3,2,1,0:T(8,128)}, u32[]{:S(2)}) copy-start(f32[1,1,128,256]{3,2,1,0:T(8,128)} %param.5) | copy-start | bytes 393220
  7.2 69.1 %all-gather.5.cloned.1.call-start = ((), (), s32[]{:S(2)}) async-start(), calls=%async_computation.2 | async-start | bytes 2359296 | tf_op jit(solution)/shard_map/all_gather | solution.py:38
  33.9 0.7 copy-start.1
  64.1 35.3 %reduce-scatter.2.cloned.1.call-start = ((), (), s32[]{:S(2)}) async-start(), calls=%async_computation.3 | async-start | bytes 1179648 | tf_op jit(solution)/shard_map/reduce_scatter | solution.py:46
  70.4 29.2 %copy-start.3 = (s32[2,4]{1,0:T(2,128)S(1)}, s32[2,4]{1,0:T(2,128)}, u32[]{:S(2)}) copy-start(s32[2,4]{1,0:T(2,128)} %param.7) | copy-start | bytes 100
  81.0 112.2 %copy-start.2 = (f32[1,128,256]{2,1,0:T(8,128)S(1)}, f32[1,128,256]{2,1,0:T(8,128)}, u32[]{:S(2)}) copy-start(f32[1,128,256]{2,1,0:T(8,128)} %copy-done.1) | copy-start | bytes 393220
  81.1 57.1 %all-gather.7.cloned.1.call-start = ((), (), s32[]{:S(2)}) async-start(), calls=%async_computation.5 | async-start | bytes 1966080 | tf_op jit(solution)/shard_map/all_gather | solution.py:53
  99.5 93.8 %all-reduce.2.cloned.1.call-start = ((), (), s32[]{:S(2)}) async-start(), calls=%async_computation.4 | async-start | bytes 524288 | tf_op jit(solution)/shard_map/psum | solution.py:58
Sparse Core Ops, SparseCore 0:
  64.2 12.0 all-gather.4
  81.2 18.2 reduce-scatter.1
  101.1 36.9 all-gather.6
  141.0 52.2 all-reduce.1
where the time goes:
time: 205 us; the launch traced here: 202 us
  waiting for transfers between devices  109 us (53%)
  blocking collectives  26.3 us (13%)
  other arithmetic  24.1 us (12%)
  matrix products  18.1 us (9%)
  between operations  16.6 us (8%)
  local copies, waits for them, and re-layouts  7.5 us (4%)
    psum x1, waiting for transfers between devices, per_device(): summed = lax.psum(diag_part, ('row', 'sub'))  50.2 us
    all_gather x1, waiting for transfers between devices, per_device(): collected = lax.all_gather(reduced[:, None], 'row', axis=1, tiled=True)  34.6 us
    another operation x3, other arithmetic, per_device(): lax.linalg.triangular_solve(diag_factor, identity, left_side=True, lower=...  20.6 us
    reduce_scatter x1, waiting for transfers between devices, per_device(): lax.psum_scatter(jnp.einsum('kihmx,kmxy->kihy', selected, blocks, precisi...  18.3 us
    all_gather x1, blocking collectives, per_device(): whole_panel = lax.all_gather(update, 'row', axis=1, tiled=True)  15.3 us
    all_to_all x1, blocking collectives, per_device(): lax.all_to_all(outgoing, 'col', split_axis=0, concat_axis=0, tiled=True)  11 us
    all_gather x1, waiting for transfers between devices, per_device(): blocks = lax.all_gather(incoming, 'sub', axis=3, tiled=True)  5.95 us
    dot_general x1, matrix products, per_device(): jnp.einsum('kmj,ihjx->kihmx', spread_map, parent_local, precision=HIGHEST)  5.8 us
  transfers between devices with their start and end apart: 4, of which 4 were waited for; matrix products, arithmetic and copies ran while one was open for 5% of the time, Pallas kernels for 0%

commit v1 on v0

v1 whole, which is shorter than its diff:
```python
import functools
import jax
import jax.numpy as jnp
from jax import lax
from jax.experimental import pallas as pl
from jax.experimental.pallas import tpu as pltpu
from jax.sharding import PartitionSpec as P

HIGHEST = lax.Precision.HIGHEST
MESH = pl.DeviceIdType.MESH
F32 = jnp.float32
BF16 = jnp.bfloat16


def split(x):
    hi = x.astype(BF16)
    return hi, (x - hi.astype(F32)).astype(BF16)


def dot3(a, b, dims=((1,), (0,))):
    def one(x, y):
        return lax.dot_general(x, y, (dims, ((), ())), preferred_element_type=F32)

    return one(a[0], b[0]) + (one(a[0], b[1]) + one(a[1], b[0]))


def dot6(a, b):
    return jnp.dot(a, b, precision=HIGHEST, preferred_element_type=F32)


def invert_lower(tri):
    size = tri.shape[0]
    row = lax.broadcasted_iota(jnp.int32, (size, size), 0)
    col = lax.broadcasted_iota(jnp.int32, (size, size), 1)
    on_diag = row == col
    only = jnp.where(on_diag, tri, 0.0)
    by_col = 1.0 / jnp.sum(only, axis=0, keepdims=True)
    by_row = 1.0 / jnp.sum(only, axis=1, keepdims=True)

    def below(m):
        same = (row // (2 * m)) == (col // (2 * m))
        return same & ((row // m) % 2 == 1) & ((col // m) % 2 == 0)

    inv = jnp.where(on_diag, by_row, 0.0) - jnp.where(below(1), tri * by_row * by_col, 0.0)
    m = 2
    while m < size:
        inv = inv - dot6(inv, dot6(jnp.where(below(m), tri, 0.0), inv))
        m *= 2
    return inv


def kernel(R, C, *refs):
    front, parent, panel, factor, cross_out, diag_out = refs[:6]
    pk = refs[6 : 6 + C]
    (s_hi, s_lo, inv_hi, inv_lo, ysend, yrecv, w, wsend, wrecv, macc, mrecv, mhalf, mpart, gall,
     main_s, main_r, sub_s, sub_r, y_s, y_r, w_s, w_r, ms_s, ms_r, m_s, m_r, g_s, g_r, gs_s, gs_r) = refs[6 + C :]
    half = panel.shape[0]
    width = panel.shape[1]
    par_rows = w.shape[0]
    front_len = front.shape[1]
    slots = front_len // C + 1
    piece = half // R
    r = lax.axis_index("row")
    c = lax.axis_index("col")
    s = lax.axis_index("sub")
    other = 1 - s

    def rowat(d):
        return lax.rem(r + d + R, R)

    def colat(e):
        return lax.rem(c + e + C, C)

    barrier = pltpu.get_barrier_semaphore()
    for d in range(1, R):
        pl.semaphore_signal(barrier, inc=1, device_id={"row": rowat(d)}, device_id_type=MESH)
    for e in range(1, C):
        pl.semaphore_signal(barrier, inc=1, device_id={"col": colat(e)}, device_id_type=MESH)
    pl.semaphore_signal(barrier, inc=1, device_id={"sub": other}, device_id_type=MESH)
    pl.semaphore_wait(barrier, R - 1 + C - 1 + 1)

    started = []

    def send(src, dst, ssem, rsem, dev):
        copy = pltpu.make_async_remote_copy(
            src_ref=src, dst_ref=dst, send_sem=ssem, recv_sem=rsem, device_id=dev, device_id_type=MESH
        )
        copy.start()
        started.append(copy)

    def arrived(dst, ssem, rsem):
        pltpu.make_async_remote_copy(
            src_ref=dst, dst_ref=dst, send_sem=ssem, recv_sem=rsem, device_id={"sub": other}, device_id_type=MESH
        ).wait_recv()

    far_first = sorted(range(1, R), key=lambda d: abs(d - R / 2))
    near_first = far_first[::-1]

    pk[0][r, s] = panel[...]
    own = pk[0].at[r, s]
    for d in far_first:
        send(own, own, main_s.at[d], main_r.at[d], {"row": rowat(d)})
    for e in range(1, C):
        send(own, pk[e].at[r, s], main_s.at[e * R], main_r.at[e * R], {"col": colat(e)})
    send(own, own, sub_s.at[0], sub_r.at[0], {"sub": other})

    for j in range(parent.shape[0]):
        hi, lo = split(parent[j])
        s_hi[j] = hi
        s_lo[j] = lo

    def take_row(d):
        block = pk[0].at[rowat(-d), s]
        arrived(block, main_s.at[d], main_r.at[d])
        for e in range(1, C):
            key = e * R + d
            send(block, pk[e].at[rowat(-d), s], main_s.at[key], main_r.at[key], {"col": colat(e)})
        send(block, block, sub_s.at[d], sub_r.at[d], {"sub": other})

    def take_col(e, d):
        block = pk[e].at[rowat(-d), s]
        key = e * R + d
        arrived(block, main_s.at[key], main_r.at[key])
        send(block, block, sub_s.at[key], sub_r.at[key], {"sub": other})

    def take_sub(e, d):
        key = e * R + d
        arrived(pk[e].at[rowat(-d), other], sub_s.at[key], sub_r.at[key])

    for d in near_first:
        take_row(d)

    h = width // 2
    tri = factor[...]
    top = invert_lower(tri[:h, :h])
    low = invert_lower(tri[h:, h:])
    corner = -dot6(low, dot6(tri[h:, :h], top))
    inverse = jnp.concatenate(
        [jnp.concatenate([top, jnp.zeros((h, h), F32)], axis=1), jnp.concatenate([corner, low], axis=1)], axis=0
    )
    hi, lo = split(inverse)
    inv_hi[...] = hi
    inv_lo[...] = lo

    for d in [0] + near_first:
        for e in range(1, C):
            take_col(e, d)

    def product(e):
        kid = colat(-e)
        count = jnp.int32(0)
        which = [jnp.int32(0)] * slots
        column = [jnp.int32(0)] * slots
        for b in range(front_len):
            f = front[kid, b]
            hit = lax.rem(f, C) == c
            for m in range(slots):
                here = hit & (count == m)
                which[m] = jnp.where(here, b, which[m])
                column[m] = jnp.where(here, lax.div(f, C), column[m])
            count = count + hit.astype(jnp.int32)
        total = None
        for m in range(slots):
            used = jnp.where(count > m, 1.0, 0.0).astype(F32)
            block = pk[e][which[m]].reshape(2 * half, width) * used
            term = dot3((s_hi[column[m]], s_lo[column[m]]), split(block))
            total = term if total is None else total + term
        return total.reshape(par_rows, half, width)

    for d in range(R):
        take_sub(0, d)
    w[...] = product(0)
    for e in range(1, C):
        for d in range(R):
            take_sub(e, d)
        ysend[e - 1] = product(e)
        send(ysend.at[e - 1], yrecv.at[e - 1], y_s.at[e - 1], y_r.at[e - 1], {"col": colat(-e)})
    for e in range(1, C):
        arrived(yrecv.at[e - 1], y_s.at[e - 1], y_r.at[e - 1])
        w[...] = w[...] + yrecv[e - 1]

    lhs = []
    for p in range(par_rows):
        which = jnp.int32(0)
        used = jnp.float32(0.0)
        for a in range(front_len):
            here = front[c, a] == p * R + r
            which = jnp.where(here, a, which)
            used = jnp.where(here, 1.0, used)
        lhs.append(pk[0][which, s] * used)
    lhs = jnp.concatenate(lhs, axis=0)
    macc[...] = dot3(split(lhs), split(w[...].reshape(par_rows * half, width)), ((0,), (0,))).reshape(2, half, width)
    send(macc.at[other], mrecv, ms_s.at[0], ms_r.at[0], {"sub": other})

    for d in far_first + [0]:
        wsend[d] = w[lax.div(front[c, rowat(d)], R)]
        if d:
            send(wsend.at[d], wrecv.at[d], w_s.at[d], w_r.at[d], {"row": rowat(d)})
    wrecv[0] = wsend[0]

    arrived(mrecv, ms_s.at[0], ms_r.at[0])
    mhalf[...] = (macc[s] + mrecv[...]).reshape(R, piece, width)
    for d in far_first:
        send(mhalf.at[rowat(d)], mpart.at[d], m_s.at[d], m_r.at[d], {"row": rowat(d)})
    total = mhalf[r]
    for d in near_first:
        arrived(mpart.at[d], m_s.at[d], m_r.at[d])
        total = total + mpart[d]
    row = lax.broadcasted_iota(jnp.int32, (piece, width), 0) + (s * half + r * piece)
    col = lax.broadcasted_iota(jnp.int32, (piece, width), 1)
    total = total + jnp.where(row == col, 1.0, 0.0)
    inv_pair = (inv_hi[...], inv_lo[...])
    gall[s, r] = dot3(split(total), inv_pair)
    mine = gall.at[s, r]
    for d in far_first:
        send(mine, mine, g_s.at[d], g_r.at[d], {"row": rowat(d)})
    send(mine, mine, gs_s.at[0], gs_r.at[0], {"sub": other})
    for d in near_first:
        block = gall.at[s, rowat(-d)]
        arrived(block, g_s.at[d], g_r.at[d])
        send(block, block, gs_s.at[d], gs_r.at[d], {"sub": other})

    for d in near_first:
        arrived(wrecv.at[d], w_s.at[d], w_r.at[d])
    owner = lax.rem(front[c, r], R)
    picked = wrecv[lax.rem(r - owner + R, R)]
    cross_out[...] = -dot3(split(picked), inv_pair)

    for d in range(R):
        arrived(gall.at[other, rowat(-d)], gs_s.at[d], gs_r.at[d])
    diag_out[...] = dot3(inv_pair, split(gall[...].reshape(2 * half, width)), ((0,), (0,)))

    for copy in started:
        copy.wait_send()


def per_device(R, C, sigma_parent, panel, diag_factor, frontier):
    half, width = panel.shape[2:]
    par_rows, par_cols = sigma_parent.shape[0], sigma_parent.shape[3]
    front_len = frontier.shape[1]
    parent = sigma_parent.reshape(par_rows, half, par_cols, width)
    parent = parent.transpose(2, 0, 1, 3).reshape(par_cols, par_rows * half, width)
    vm = pltpu.VMEM
    dma = pltpu.SemaphoreType.DMA
    side = max(C - 1, 1)
    piece = half // R
    scratch = [vm((front_len, 2, half, width), F32) for _ in range(C)] + [
        vm((par_cols, par_rows * half, width), BF16),
        vm((par_cols, par_rows * half, width), BF16),
        vm((width, width), BF16),
        vm((width, width), BF16),
        vm((side, par_rows, half, width), F32),
        vm((side, par_rows, half, width), F32),
        vm((par_rows, half, width), F32),
        vm((R, half, width), F32),
        vm((R, half, width), F32),
        vm((2, half, width), F32),
        vm((half, width), F32),
        vm((R, piece, width), F32),
        vm((R, piece, width), F32),
        vm((2, R, piece, width), F32),
        dma((R * C,)), dma((R * C,)), dma((R * C,)), dma((R * C,)),
        dma((side,)), dma((side,)), dma((R,)), dma((R,)), dma((1,)), dma((1,)),
        dma((R,)), dma((R,)), dma((R,)), dma((R,)), dma((R,)), dma((R,)),
    ]
    spec = pl.BlockSpec(memory_space=pltpu.VMEM)
    cross, diag = pl.pallas_call(
        functools.partial(kernel, R, C),
        out_shape=(jax.ShapeDtypeStruct((half, width), F32), jax.ShapeDtypeStruct((width, width), F32)),
        in_specs=[pl.BlockSpec(memory_space=pltpu.SMEM), spec, spec, spec],
        out_specs=(spec, spec),
        scratch_shapes=scratch,
        compiler_params=pltpu.CompilerParams(
            collective_id=0, has_side_effects=True, vmem_limit_bytes=(24 if C == 2 else 58) * 2**20
        ),
    )(frontier, parent, panel.reshape(half, width), diag_factor.reshape(width, width))
    return cross.reshape(panel.shape), diag.reshape(diag_factor.shape)


def solution(mesh):
    in_specs = (
        P("grp", "row", "sub", None, "col", None),
        P(("grp", "col"), "row", "sub", None),
        P(("grp", "col"), None, None),
        P("grp", None),
    )
    out_specs = (P(("grp", "col"), "row", "sub", None), P(("grp", "col"), None, None))
    return jax.shard_map(
        functools.partial(per_device, mesh.shape["row"], mesh.shape["col"]),
        mesh=mesh, in_specs=in_specs, out_specs=out_specs, check_vma=False,
    )
```

time: 205 us -> 63.6 us (0.31); the launches traced: 202 us -> 63.4 us
  waiting for transfers between devices: 109 us -> 0 us
  Pallas kernels: 0 us -> 59.4 us
  blocking collectives: 26.3 us -> 0 us
  other arithmetic: 24.1 us -> 0 us
  matrix products: 18.1 us -> 0 us
  between operations: 16.6 us -> 0.69 us
  local copies, waits for them, and re-layouts: 7.5 us -> 3.35 us
    pallas_call x0 -> x1, Pallas kernels: none -> 59.4 us  [per_device(): pl.pallas_call(functools.partial(kernel, R, C), out_shape=(jax.ShapeDtype...]
    psum x1 -> x0, waiting for transfers between devices: 50.2 us -> none  [per_device(): summed = lax.psum(diag_part, ('row', 'sub'))]
    all_gather x2 -> x0, waiting for transfers between devices: 40.6 us -> none  [the longest x1 34.6 us: per_device(): collected = lax.all_gather(reduced[:, None], 'row', axis=1, tiled=True)]
    another operation x4 -> x0, other arithmetic: 21 us -> none  [the longest x3 20.6 us: per_device(): lax.linalg.triangular_solve(diag_factor, identity, left_side=True, lower=...]
    reduce_scatter x1 -> x0, waiting for transfers between devices: 18.3 us -> none  [per_device(): lax.psum_scatter(jnp.einsum('kihmx,kmxy->kihy', selected, blocks, precisi...]
    dot_general x7 -> x0, matrix products: 17.2 us -> none  [the longest x1 5.8 us: per_device(): jnp.einsum('kmj,ihjx->kihmx', spread_map, parent_local, precision=HIGHEST)]
    all_gather x1 -> x0, blocking collectives: 15.3 us -> none  [per_device(): whole_panel = lax.all_gather(update, 'row', axis=1, tiled=True)]
    all_to_all x1 -> x0, blocking collectives: 11 us -> none  [per_device(): lax.all_to_all(outgoing, 'col', split_axis=0, concat_axis=0, tiled=True)]
  transfers between devices with their start and end apart: 4 -> 0, of which waited for: 4 -> 0; matrix products, arithmetic and copies ran while one was open for 5% -> 0% of each run, Pallas kernels for 0% -> 0%
where the time goes in v1:
time: 63.6 us; the launch traced here: 63.4 us
  Pallas kernels  59.4 us (93%)
  local copies, waits for them, and re-layouts  3.35 us (5%)
  between operations  0.69 us (1%)
    pallas_call x1, Pallas kernels, per_device(): pl.pallas_call(functools.partial(kernel, R, C), out_shape=(jax.ShapeDtype...  59.4 us
    transpose x1, local copies, waits for them, and re-layouts, per_device(): parent.transpose(2, 0, 1, 3).reshape(par_cols, par_rows * half, width)  1.98 us
    unnamed x8, local copies, waits for them, and re-layouts  1.37 us

profile of v1, /device:TPU:1, one launch (start us, length us, event | category | flops | bytes accessed | tf_op | source)
XLA Modules:
  0.0 63.4 jit_solution(15866185002530015019)
XLA Ops:
  0.6 0.0 copy-start
  0.6 0.0 copy-start.1
  0.7 0.0 copy-start.2
  0.7 2.0 %copy.9 = f32[3,1,128,6,1,256]{5,2,0,3,1,4:T(8,128)S(1)} copy(f32[3,1,128,6,1,256]{5,4,3,2,1,0:T(1,128)} %param.4) | data formatting | bytes 4718592 | tf_op jit(solution)/shard_map/transpose | solution.py:242
  2.6 0.0 copy-done
  2.7 0.0 copy-done.1
  2.7 0.0 copy-done.2
  2.7 59.4 %shard_map.59 = (f32[128,256]{1,0:T(8,128)S(1)}, f32[256,256]{1,0:T(8,128)S(1)}) custom-call(s32[2,4]{1,0:T(2,128)S(1)} %copy-done.2, f32[6,384,256]{2,1,0:T(8,128)S(1)} %bitcast.9, f32[128,256]{1,0:T(8,128)S(1)} %bitcast.12, f32[256,256]{1,0:T(8,128)S(1)} %bitcast.10), custom_call_target="tpu_custom_call" | custom-call | tf_op jit(solution)/shard_map/pallas_call | solution.py:267
  62.1 0.7 %copy.12 = f32[1,1,128,256]{3,2,1,0:T(8,128)} copy(f32[1,1,128,256]{3,2,1,0:T(8,128)S(1)} %bitcast.13) | data formatting | bytes 262144
  62.7 0.7 %copy.13 = f32[1,256,256]{2,1,0:T(8,128)} copy(f32[1,256,256]{2,1,0:T(8,128)S(1)} %bitcast.11) | data formatting | bytes 524288
Async XLA Ops:
  0.6 2.0 %copy-start = (f32[1,256,256]{2,1,0:T(8,128)S(1)}, f32[1,256,256]{2,1,0:T(8,128)}, u32[]{:S(2)}) copy-start(f32[1,256,256]{2,1,0:T(8,128)} %param.6) | copy-start | bytes 786436
  0.6 2.0 %copy-start.1 = (f32[1,1,128,256]{3,2,1,0:T(8,128)S(1)}, f32[1,1,128,256]{3,2,1,0:T(8,128)}, u32[]{:S(2)}) copy-start(f32[1,1,128,256]{3,2,1,0:T(8,128)} %param.5) | copy-start | bytes 393220
  0.7 2.0 %copy-start.2 = (s32[2,4]{1,0:T(2,128)S(1)}, s32[2,4]{1,0:T(2,128)}, u32[]{:S(2)}) copy-start(s32[2,4]{1,0:T(2,128)} %refs_0_.1) | copy-start | bytes 100

commit v2 on v1

v2 whole, which is shorter than its diff:
```python
import functools
import jax
import jax.numpy as jnp
from jax import lax
from jax.experimental import pallas as pl
from jax.experimental.pallas import tpu as pltpu
from jax.sharding import PartitionSpec as P

HIGHEST = lax.Precision.HIGHEST
MESH = pl.DeviceIdType.MESH
F32 = jnp.float32
BF16 = jnp.bfloat16


def split(x):
    hi = x.astype(BF16)
    return hi, (x - hi.astype(F32)).astype(BF16)


def dot3(a, b, dims=((1,), (0,))):
    def one(x, y):
        return lax.dot_general(x, y, (dims, ((), ())), preferred_element_type=F32)

    return one(a[0], b[0]) + (one(a[0], b[1]) + one(a[1], b[0]))


def dot6(a, b):
    return jnp.dot(a, b, precision=HIGHEST, preferred_element_type=F32)


def invert_steps(tri):
    size = tri.shape[0]
    row = lax.broadcasted_iota(jnp.int32, (size, size), 0)
    col = lax.broadcasted_iota(jnp.int32, (size, size), 1)
    on_diag = row == col
    only = jnp.where(on_diag, tri, 0.0)
    by_col = 1.0 / jnp.sum(only, axis=0, keepdims=True)
    by_row = 1.0 / jnp.sum(only, axis=1, keepdims=True)

    def below(m):
        same = (row // (2 * m)) == (col // (2 * m))
        return same & ((row // m) % 2 == 1) & ((col // m) % 2 == 0)

    inv = jnp.where(on_diag, by_row, 0.0) - jnp.where(below(1), tri * by_row * by_col, 0.0)
    yield inv
    m = 2
    while m < size:
        inv = inv - dot6(inv, dot6(jnp.where(below(m), tri, 0.0), inv))
        m *= 2
        yield inv


CH = 2


def kernel(R, C, *refs):
    refs = list(refs)
    front, parent, panel, factor, cross_out, diag_out = refs[:6]
    del refs[:6]
    pk = [[refs.pop(0) for _ in range(CH)] for _ in range(C)]
    w = [refs.pop(0) for _ in range(CH)]
    wsend = [refs.pop(0) for _ in range(CH)]
    wrecv = [refs.pop(0) for _ in range(CH)]
    (s_hi, s_lo, inv_hi, inv_lo, ysend, yrecv, macc, mrecv, mhalf, mpart, gall,
     z_s, z_r, x_s, x_r, sub_s, sub_r, y_s, y_r, w_s, w_r, ms_s, ms_r, m_s, m_r, g_s, g_r, gs_s, gs_r) = refs
    half = panel.shape[0]
    width = panel.shape[1]
    wide = width // CH
    par_rows = w[0].shape[0]
    front_len = front.shape[1]
    slots = front_len // C + 1
    piece = half // R
    r = lax.axis_index("row")
    c = lax.axis_index("col")
    s = lax.axis_index("sub")
    other = 1 - s

    def rowat(d):
        return lax.rem(r + d + R, R)

    def colat(e):
        return lax.rem(c + e + C, C)

    barrier = pltpu.get_barrier_semaphore()
    for d in range(1, R):
        pl.semaphore_signal(barrier, inc=1, device_id={"row": rowat(d)}, device_id_type=MESH)
    for e in range(1, C):
        pl.semaphore_signal(barrier, inc=1, device_id={"col": colat(e)}, device_id_type=MESH)
    pl.semaphore_signal(barrier, inc=1, device_id={"sub": other}, device_id_type=MESH)
    pl.semaphore_wait(barrier, R - 1 + C - 1 + 1)

    started = []

    def remote(src, dst, ssem, rsem, dev):
        return pltpu.make_async_remote_copy(
            src_ref=src, dst_ref=dst, send_sem=ssem, recv_sem=rsem, device_id=dev, device_id_type=MESH
        )

    def send(src, dst, ssem, rsem, dev, cond=None):
        def go():
            remote(src, dst, ssem, rsem, dev).start()

        def done():
            remote(src, dst, ssem, rsem, dev).wait_send()

        when(cond, go)
        started.append((cond, done))

    def when(cond, body):
        if cond is None:
            body()
        else:
            pl.when(cond)(body)

    def arrived(dst, ssem, rsem):
        remote(dst, dst, ssem, rsem, {"sub": other}).wait_recv()

    far_first = sorted(range(1, R), key=lambda d: abs(d - R / 2))
    near_first = far_first[::-1]

    def key(way, t, ch):
        return (way * R + t) * CH + ch

    keys = 2 * R * CH

    def source(way, t):
        return r - t if way == 0 else r + t

    def from_row(way, t):
        if t == 0:
            return None
        return r >= t if way == 0 else r + t <= R - 1

    def both(a, b):
        return b if a is None else a & b

    def pass_on(way, t, ch):
        here = from_row(way, t)
        block = pk[0][ch].at[source(way, t), s]
        if t + 1 < R:
            for side in (0, 1) if t == 0 else (way,):
                k = key(side, t + 1, ch)
                inside = r < R - 1 if side == 0 else r > 0
                send(block, block, z_s.at[k], z_r.at[k], {"row": r + 1 if side == 0 else r - 1}, both(here, inside))
        k = key(way, t, ch)
        for e in range(1, C):
            q = (e - 1) * keys + k
            send(block, pk[e][ch].at[source(way, t), s], x_s.at[q], x_r.at[q], {"col": colat(e)}, here)
        send(block, block, sub_s.at[k], sub_r.at[k], {"sub": other}, here)

    def take_row(way, t, ch):
        k = key(way, t, ch)
        when(from_row(way, t), lambda: arrived(pk[0][ch].at[source(way, t), s], z_s.at[k], z_r.at[k]))
        pass_on(way, t, ch)

    def take_col(e, way, t, ch):
        q = (e - 1) * keys + key(way, t, ch)
        here = from_row(way, t)
        block = pk[e][ch].at[source(way, t), s]
        when(here, lambda: arrived(block, x_s.at[q], x_r.at[q]))
        q += keys
        send(block, block, sub_s.at[q], sub_r.at[q], {"sub": other}, here)

    def take_sub(e, way, t, ch):
        q = e * keys + key(way, t, ch)
        when(from_row(way, t), lambda: arrived(pk[e][ch].at[source(way, t), other], sub_s.at[q], sub_r.at[q]))

    h = width // 2
    tri = factor[...]
    steps = [invert_steps(tri[:h, :h]), invert_steps(tri[h:, h:])]
    blocks = [None, None]

    def advance(count=1):
        for _ in range(count):
            for i in range(2):
                blocks[i] = next(steps[i], blocks[i])

    for ch in range(CH):
        pk[0][ch][r, s] = panel[:, ch * wide : (ch + 1) * wide]
        pass_on(0, 0, ch)

    for j in range(parent.shape[0]):
        hi, lo = split(parent[j])
        s_hi[j] = hi
        s_lo[j] = lo

    for t in range(1, R):
        for ch in range(CH):
            take_row(0, t, ch)
            take_row(1, t, ch)
        for ch in range(CH):
            for e in range(1, C):
                for way in (0,) if t == 1 else (0, 1):
                    take_col(e, way, t - 1, ch)
        if t < 3:
            advance()

    def product(e, ch):
        kid = colat(-e)
        count = jnp.int32(0)
        which = [jnp.int32(0)] * slots
        column = [jnp.int32(0)] * slots
        for b in range(front_len):
            f = front[kid, b]
            hit = lax.rem(f, C) == c
            for m in range(slots):
                here = hit & (count == m)
                which[m] = jnp.where(here, b, which[m])
                column[m] = jnp.where(here, lax.div(f, C), column[m])
            count = count + hit.astype(jnp.int32)
        total = None
        for m in range(slots):
            used = jnp.where(count > m, 1.0, 0.0).astype(F32)
            block = pk[e][ch][which[m]].reshape(2 * half, wide) * used
            term = dot3((s_hi[column[m]], s_lo[column[m]]), split(block))
            total = term if total is None else total + term
        return total.reshape(par_rows, half, wide)

    ways = [(0, 0)] + [(way, t) for t in range(1, R) for way in (0, 1)]
    for ch in range(CH):
        for e in range(1, C):
            for way in (0, 1) if R > 1 else ():
                take_col(e, way, R - 1, ch)
    for ch in range(CH):
        for e in range(1, C):
            for way, t in ways:
                take_sub(e, way, t, ch)
            n = (e - 1) * CH + ch
            ysend[n] = product(e, ch)
            send(ysend.at[n], yrecv.at[n], y_s.at[n], y_r.at[n], {"col": colat(-e)})
    for ch in range(CH):
        for way, t in ways:
            take_sub(0, way, t, ch)
    for ch in range(CH):
        w[ch][...] = product(0, ch)

    lhs = []
    for p in range(par_rows):
        which = jnp.int32(0)
        used = jnp.float32(0.0)
        for a in range(front_len):
            here = front[c, a] == p * R + r
            which = jnp.where(here, a, which)
            used = jnp.where(here, 1.0, used)
        lhs.append(jnp.concatenate([pk[0][ch][which, s] for ch in range(CH)], axis=1) * used)
    lhs = split(jnp.concatenate(lhs, axis=0))
    advance(3)

    def rows_out(ch):
        for e in range(1, C):
            n = (e - 1) * CH + ch
            arrived(yrecv.at[n], y_s.at[n], y_r.at[n])
            w[ch][...] = w[ch][...] + yrecv[n]
        macc[ch] = dot3(lhs, split(w[ch][...].reshape(par_rows * half, wide)), ((0,), (0,))).reshape(2, half, wide)
        send(macc.at[ch, other], mrecv.at[ch], ms_s.at[ch], ms_r.at[ch], {"sub": other})
        for d in far_first + [0]:
            wsend[ch][d] = w[ch][lax.div(front[c, rowat(d)], R)]
            if d:
                k = ch * R + d
                send(wsend[ch].at[d], wrecv[ch].at[d], w_s.at[k], w_r.at[k], {"row": rowat(d)})
        wrecv[ch][0] = wsend[ch][0]

    def diag_out_part(ch):
        arrived(mrecv.at[ch], ms_s.at[ch], ms_r.at[ch])
        mhalf[ch] = (macc[ch, s] + mrecv[ch]).reshape(R, piece, wide)
        for d in far_first:
            k = ch * R + d
            send(mhalf.at[ch, rowat(d)], mpart.at[ch, d], m_s.at[k], m_r.at[k], {"row": rowat(d)})

    for ch in range(CH):
        rows_out(ch)
        diag_out_part(ch)

    advance(8)
    top, low = blocks
    corner = -dot6(low, dot6(tri[h:, :h], top))
    inverse = jnp.concatenate(
        [jnp.concatenate([top, jnp.zeros((h, h), F32)], axis=1), jnp.concatenate([corner, low], axis=1)], axis=0
    )
    hi, lo = split(inverse)
    inv_hi[...] = hi
    inv_lo[...] = lo
    inv_pair = (inv_hi[...], inv_lo[...])

    total = []
    for ch in range(CH):
        part = mhalf[ch, r]
        for d in near_first:
            k = ch * R + d
            arrived(mpart.at[ch, d], m_s.at[k], m_r.at[k])
            part = part + mpart[ch, d]
        total.append(part)
    total = jnp.concatenate(total, axis=1)
    row = lax.broadcasted_iota(jnp.int32, (piece, width), 0) + (s * half + r * piece)
    col = lax.broadcasted_iota(jnp.int32, (piece, width), 1)
    total = total + jnp.where(row == col, 1.0, 0.0)
    gall[s, r] = dot3(split(total), inv_pair)
    mine = gall.at[s, r]
    for d in far_first:
        send(mine, mine, g_s.at[d], g_r.at[d], {"row": rowat(d)})
    send(mine, mine, gs_s.at[0], gs_r.at[0], {"sub": other})

    picked = []
    owner = lax.rem(front[c, r], R)
    for ch in range(CH):
        for d in near_first:
            k = ch * R + d
            arrived(wrecv[ch].at[d], w_s.at[k], w_r.at[k])
        picked.append(wrecv[ch][lax.rem(r - owner + R, R)])
    cross_out[...] = -dot3(split(jnp.concatenate(picked, axis=1)), inv_pair)

    for d in near_first:
        block = gall.at[s, rowat(-d)]
        arrived(block, g_s.at[d], g_r.at[d])
        send(block, block, gs_s.at[d], gs_r.at[d], {"sub": other})
    for d in range(R):
        arrived(gall.at[other, rowat(-d)], gs_s.at[d], gs_r.at[d])
    diag_out[...] = dot3(inv_pair, split(gall[...].reshape(2 * half, width)), ((0,), (0,)))

    for cond, done in started:
        when(cond, done)


def per_device(R, C, sigma_parent, panel, diag_factor, frontier):
    half, width = panel.shape[2:]
    par_rows, par_cols = sigma_parent.shape[0], sigma_parent.shape[3]
    front_len = frontier.shape[1]
    parent = sigma_parent.reshape(par_rows, half, par_cols, width)
    parent = parent.transpose(2, 0, 1, 3).reshape(par_cols, par_rows * half, width)
    vm = pltpu.VMEM
    dma = pltpu.SemaphoreType.DMA
    side = max(C - 1, 1)
    piece = half // R
    wide = width // CH
    keys = 2 * R * CH
    scratch = (
        [vm((front_len, 2, half, wide), F32) for _ in range(C * CH)]
        + [vm((par_rows, half, wide), F32) for _ in range(CH)]
        + [vm((R, half, wide), F32) for _ in range(2 * CH)]
        + [
            vm((par_cols, par_rows * half, width), BF16),
            vm((par_cols, par_rows * half, width), BF16),
            vm((width, width), BF16),
            vm((width, width), BF16),
            vm((side * CH, par_rows, half, wide), F32),
            vm((side * CH, par_rows, half, wide), F32),
            vm((CH, 2, half, wide), F32),
            vm((CH, half, wide), F32),
            vm((CH, R, piece, wide), F32),
            vm((CH, R, piece, wide), F32),
            vm((2, R, piece, width), F32),
        ]
        + [dma((keys,))] * 2 + [dma((side * keys,))] * 2 + [dma((C * keys,))] * 2
        + [dma((side * CH,))] * 2 + [dma((CH * R,))] * 2 + [dma((CH,))] * 2 + [dma((CH * R,))] * 2
        + [dma((R,))] * 4
    )
    spec = pl.BlockSpec(memory_space=pltpu.VMEM)
    cross, diag = pl.pallas_call(
        functools.partial(kernel, R, C),
        out_shape=(jax.ShapeDtypeStruct((half, width), F32), jax.ShapeDtypeStruct((width, width), F32)),
        in_specs=[pl.BlockSpec(memory_space=pltpu.SMEM), spec, spec, spec],
        out_specs=(spec, spec),
        scratch_shapes=scratch,
        compiler_params=pltpu.CompilerParams(
            collective_id=0, has_side_effects=True, vmem_limit_bytes=(24 if C == 2 else 58) * 2**20
        ),
    )(frontier, parent, panel.reshape(half, width), diag_factor.reshape(width, width))
    return cross.reshape(panel.shape), diag.reshape(diag_factor.shape)


def solution(mesh):
    in_specs = (
        P("grp", "row", "sub", None, "col", None),
        P(("grp", "col"), "row", "sub", None),
        P(("grp", "col"), None, None),
        P("grp", None),
    )
    out_specs = (P(("grp", "col"), "row", "sub", None), P(("grp", "col"), None, None))
    return jax.shard_map(
        functools.partial(per_device, mesh.shape["row"], mesh.shape["col"]),
        mesh=mesh, in_specs=in_specs, out_specs=out_specs, check_vma=False,
    )
```

time: 63.6 us -> 53.8 us (0.85)
  Pallas kernels: 59.4 us -> 49.6 us
    pallas_call x1, Pallas kernels: 59.4 us -> 49.6 us  [per_device(): pl.pallas_call(functools.partial(kernel, R, C), out_shape=(jax.ShapeDtype...]
where the time goes in v2:
time: 53.8 us; the launch traced here: 53.6 us
  Pallas kernels  49.6 us (92%)
  local copies, waits for them, and re-layouts  3.35 us (6%)
  between operations  0.69 us (1%)
    pallas_call x1, Pallas kernels, per_device(): pl.pallas_call(functools.partial(kernel, R, C), out_shape=(jax.ShapeDtype...  49.6 us
    transpose x1, local copies, waits for them, and re-layouts, per_device(): parent.transpose(2, 0, 1, 3).reshape(par_cols, par_rows * half, width)  1.98 us
    unnamed x8, local copies, waits for them, and re-layouts  1.37 us

profile of v2, /device:TPU:1, one launch (start us, length us, event | category | flops | bytes accessed | tf_op | source)
XLA Modules:
  0.0 53.6 jit_solution(2134474161109867060)
XLA Ops:
  0.6 0.0 copy-start
  0.6 0.0 copy-start.1
  0.7 0.0 copy-start.2
  0.7 2.0 %copy.9 = f32[3,1,128,6,1,256]{5,2,0,3,1,4:T(8,128)S(1)} copy(f32[3,1,128,6,1,256]{5,4,3,2,1,0:T(1,128)} %param.4) | data formatting | bytes 4718592 | tf_op jit(solution)/shard_map/transpose | solution.py:329
  2.6 0.0 copy-done
  2.7 0.0 copy-done.1
  2.7 0.0 copy-done.2
  2.7 49.6 %shard_map.59 = (f32[128,256]{1,0:T(8,128)S(1)}, f32[256,256]{1,0:T(8,128)S(1)}) custom-call(s32[2,4]{1,0:T(2,128)S(1)} %copy-done.2, f32[6,384,256]{2,1,0:T(8,128)S(1)} %bitcast.9, f32[128,256]{1,0:T(8,128)S(1)} %bitcast.12, f32[256,256]{1,0:T(8,128)S(1)} %bitcast.10), custom_call_target="tpu_custom_call" | custom-call | tf_op jit(solution)/shard_map/pallas_call | solution.py:358
  52.3 0.7 %copy.12 = f32[1,1,128,256]{3,2,1,0:T(8,128)} copy(f32[1,1,128,256]{3,2,1,0:T(8,128)S(1)} %bitcast.13) | data formatting | bytes 262144
  52.9 0.7 %copy.13 = f32[1,256,256]{2,1,0:T(8,128)} copy(f32[1,256,256]{2,1,0:T(8,128)S(1)} %bitcast.11) | data formatting | bytes 524288
Async XLA Ops:
  0.6 2.0 %copy-start = (f32[1,256,256]{2,1,0:T(8,128)S(1)}, f32[1,256,256]{2,1,0:T(8,128)}, u32[]{:S(2)}) copy-start(f32[1,256,256]{2,1,0:T(8,128)} %param.6) | copy-start | bytes 786436
  0.6 2.0 %copy-start.1 = (f32[1,1,128,256]{3,2,1,0:T(8,128)S(1)}, f32[1,1,128,256]{3,2,1,0:T(8,128)}, u32[]{:S(2)}) copy-start(f32[1,1,128,256]{3,2,1,0:T(8,128)} %param.5) | copy-start | bytes 393220
  0.7 2.0 %copy-start.2 = (s32[2,4]{1,0:T(2,128)S(1)}, s32[2,4]{1,0:T(2,128)}, u32[]{:S(2)}) copy-start(s32[2,4]{1,0:T(2,128)} %refs_0_.1) | copy-start | bytes 100

commit v3 on v2

--- a/solution.py
+++ b/solution.py
@@ -219,9 +219,8 @@
     ways = [(0, 0)] + [(way, t) for t in range(1, R) for way in (0, 1)]
     for ch in range(CH):
         for e in range(1, C):
-            for way in (0, 1) if R > 1 else ():
+            for way in (0, 1):
                 take_col(e, way, R - 1, ch)
-    for ch in range(CH):
         for e in range(1, C):
             for way, t in ways:
                 take_sub(e, way, t, ch)
@@ -244,32 +243,6 @@
             used = jnp.where(here, 1.0, used)
         lhs.append(jnp.concatenate([pk[0][ch][which, s] for ch in range(CH)], axis=1) * used)
     lhs = split(jnp.concatenate(lhs, axis=0))
-    advance(3)
-
-    def rows_out(ch):
-        for e in range(1, C):
-            n = (e - 1) * CH + ch
-            arrived(yrecv.at[n], y_s.at[n], y_r.at[n])
-            w[ch][...] = w[ch][...] + yrecv[n]
-        macc[ch] = dot3(lhs, split(w[ch][...].reshape(par_rows * half, wide)), ((0,), (0,))).reshape(2, half, wide)
-        send(macc.at[ch, other], mrecv.at[ch], ms_s.at[ch], ms_r.at[ch], {"sub": other})
-        for d in far_first + [0]:
-            wsend[ch][d] = w[ch][lax.div(front[c, rowat(d)], R)]
-            if d:
-                k = ch * R + d
-                send(wsend[ch].at[d], wrecv[ch].at[d], w_s.at[k], w_r.at[k], {"row": rowat(d)})
-        wrecv[ch][0] = wsend[ch][0]
-
-    def diag_out_part(ch):
-        arrived(mrecv.at[ch], ms_s.at[ch], ms_r.at[ch])
-        mhalf[ch] = (macc[ch, s] + mrecv[ch]).reshape(R, piece, wide)
-        for d in far_first:
-            k = ch * R + d
-            send(mhalf.at[ch, rowat(d)], mpart.at[ch, d], m_s.at[k], m_r.at[k], {"row": rowat(d)})
-
-    for ch in range(CH):
-        rows_out(ch)
-        diag_out_part(ch)
 
     advance(8)
     top, low = blocks
@@ -281,6 +254,38 @@
     inv_hi[...] = hi
     inv_lo[...] = lo
     inv_pair = (inv_hi[...], inv_lo[...])
+
+    def rows_out(ch):
+        for e in range(1, C):
+            n = (e - 1) * CH + ch
+            arrived(yrecv.at[n], y_s.at[n], y_r.at[n])
+            w[ch][...] = w[ch][...] + yrecv[n]
+        macc[ch] = dot3(lhs, split(w[ch][...].reshape(par_rows * half, wide)), ((0,), (0,))).reshape(2, half, wide)
+        send(macc.at[ch, other], mrecv.at[ch], ms_s.at[ch], ms_r.at[ch], {"sub": other})
+        for d in range(R):
+            wsend[ch][d] = w[ch][lax.div(front[c, rowat(d)], R)]
+
+    def rows_send(ch):
+        for d in far_first:
+            if d:
+                k = ch * R + d
+                send(wsend[ch].at[d], wrecv[ch].at[d], w_s.at[k], w_r.at[k], {"row": rowat(d)})
+        wrecv[ch][0] = wsend[ch][0]
+
+    def diag_out_part(ch):
+        arrived(mrecv.at[ch], ms_s.at[ch], ms_r.at[ch])
+        mhalf[ch] = (macc[ch, s] + mrecv[ch]).reshape(R, piece, wide)
+        for d in far_first:
+            k = ch * R + d
+            send(mhalf.at[ch, rowat(d)], mpart.at[ch, d], m_s.at[k], m_r.at[k], {"row": rowat(d)})
+
+    for ch in range(CH):
+        rows_out(ch)
+        if ch == 0:
+            rows_send(ch)
+        diag_out_part(ch)
+        if ch:
+            rows_send(ch)
 
     total = []
     for ch in range(CH):

time: 53.8 us -> 51.3 us (0.954)
  Pallas kernels: 49.6 us -> 47.1 us
    pallas_call x1, Pallas kernels: 49.6 us -> 47.1 us  [per_device(): pl.pallas_call(functools.partial(kernel, R, C), out_shape=(jax.ShapeDtype...]
where the time goes in v3:
time: 51.3 us; the launch traced here: 51.1 us
  Pallas kernels  47.1 us (92%)
  local copies, waits for them, and re-layouts  3.35 us (7%)
  between operations  0.69 us (1%)
    pallas_call x1, Pallas kernels, per_device(): pl.pallas_call(functools.partial(kernel, R, C), out_shape=(jax.ShapeDtype...  47.1 us
    transpose x1, local copies, waits for them, and re-layouts, per_device(): parent.transpose(2, 0, 1, 3).reshape(par_cols, par_rows * half, width)  1.98 us
    unnamed x8, local copies, waits for them, and re-layouts  1.37 us

profile of v3, /device:TPU:1, one launch (start us, length us, event | category | flops | bytes accessed | tf_op | source)
XLA Modules:
  0.0 51.1 jit_solution(2436980423447698813)
XLA Ops:
  0.6 0.0 copy-start
  0.6 0.0 copy-start.1
  0.7 0.0 copy-start.2
  0.7 2.0 %copy.9 = f32[3,1,128,6,1,256]{5,2,0,3,1,4:T(8,128)S(1)} copy(f32[3,1,128,6,1,256]{5,4,3,2,1,0:T(1,128)} %param.4) | data formatting | bytes 4718592 | tf_op jit(solution)/shard_map/transpose | solution.py:334
  2.6 0.0 copy-done
  2.7 0.0 copy-done.1
  2.7 0.0 copy-done.2
  2.7 47.1 %shard_map.59 = (f32[128,256]{1,0:T(8,128)S(1)}, f32[256,256]{1,0:T(8,128)S(1)}) custom-call(s32[2,4]{1,0:T(2,128)S(1)} %copy-done.2, f32[6,384,256]{2,1,0:T(8,128)S(1)} %bitcast.9, f32[128,256]{1,0:T(8,128)S(1)} %bitcast.12, f32[256,256]{1,0:T(8,128)S(1)} %bitcast.10), custom_call_target="tpu_custom_call" | custom-call | tf_op jit(solution)/shard_map/pallas_call | solution.py:363
  49.8 0.7 %copy.12 = f32[1,1,128,256]{3,2,1,0:T(8,128)} copy(f32[1,1,128,256]{3,2,1,0:T(8,128)S(1)} %bitcast.13) | data formatting | bytes 262144
  50.4 0.7 %copy.13 = f32[1,256,256]{2,1,0:T(8,128)} copy(f32[1,256,256]{2,1,0:T(8,128)S(1)} %bitcast.11) | data formatting | bytes 524288
Async XLA Ops:
  0.6 2.0 %copy-start = (f32[1,256,256]{2,1,0:T(8,128)S(1)}, f32[1,256,256]{2,1,0:T(8,128)}, u32[]{:S(2)}) copy-start(f32[1,256,256]{2,1,0:T(8,128)} %param.6) | copy-start | bytes 786436
  0.6 2.0 %copy-start.1 = (f32[1,1,128,256]{3,2,1,0:T(8,128)S(1)}, f32[1,1,128,256]{3,2,1,0:T(8,128)}, u32[]{:S(2)}) copy-start(f32[1,1,128,256]{3,2,1,0:T(8,128)} %param.5) | copy-start | bytes 393220
  0.7 2.0 %copy-start.2 = (s32[2,4]{1,0:T(2,128)S(1)}, s32[2,4]{1,0:T(2,128)}, u32[]{:S(2)}) copy-start(s32[2,4]{1,0:T(2,128)} %refs_0_.1) | copy-start | bytes 100
